TPU v7x, 128 devices: a whole 4x4x4 slice. The times are simulated.
128 devices in a mesh: fsdp: 8 (over x, core), tp: 16 (over y, z).
Axes of the slice: x: 4, y: 4, z: 4, core: 2. Of those that a mesh axis runs over, the one named last changes fastest.
Arguments:
- grad: bfloat16 [3072, 16384], P('fsdp', 'tp'), may hold values from -0.375 to 0.375
- left_stat: float32 [128, 1024, 1024], P(('fsdp', 'tp')), as said below
- right_stat: float32 [128, 1024, 1024], P(('fsdp', 'tp')), as said below
- left_root: bfloat16 [128, 1024, 1024], P(('fsdp', 'tp')), as said below
- right_root: bfloat16 [128, 1024, 1024], P(('fsdp', 'tp')), as said below
- block_owner: int32 [48], replicated, may hold values from 0 to 127, as said below
- owner_block: int32 [128], replicated, may hold values from 0 to 47, as said below
- owner_count: int32 [128], replicated, may hold values from 0 to 1, as said below
Outputs:
- new_left: float32 [128, 1024, 1024], P(('fsdp', 'tp'))
- new_right: float32 [128, 1024, 1024], P(('fsdp', 'tp'))
- update: bfloat16 [3072, 16384], P('fsdp', 'tp')
Inputs may be any that keep to these rules, and one draw needn't show every extreme that they name: `block_owner`: the entries are distinct. Owner o is the device with fsdp index o // 16 and tp index o % 16. `owner_block`: for an owner with count 1, the block b with block_owner[b] equal to that owner; 0 for an owner with count 0. `owner_count`: 1 exactly for the owners named in block_owner. `left_stat`: Symmetric. `right_stat`: Symmetric. `left_root`: Symmetric. `right_root`: Symmetric.
All inputs are finite; a program needn't handle non-finite values.
Results may differ from a plain program's by a relative error of at most 0.0049.
Values may be sent and summed in bfloat16 or wider, within the bound.
A program may use at most 64 MiB of HBM per device.

v0:
```python
import jax
import jax.numpy as jnp
from jax import lax
from jax.sharding import PartitionSpec as P

LANE = 128


def body(grad, left_stat, right_stat, left_root, right_root, block_owner, owner_block, owner_count):
    rows_dev, block_size = grad.shape
    tp_count = lax.axis_size("tp")
    fsdp_count = lax.axis_size("fsdp")
    owners = fsdp_count * tp_count
    lane_width = LANE
    pieces_dev = rows_dev * block_size // lane_width
    sub_pieces = pieces_dev // owners
    depth = block_size // rows_dev + 2
    self_id = lax.axis_index("fsdp") * tp_count + lax.axis_index("tp")
    spread = lax.all_to_all(
        grad.reshape(owners, sub_pieces, lane_width),
        ("fsdp", "tp"),
        split_axis=0,
        concat_axis=0,
        tiled=True,
    )
    band_of_owner = owner_block // tp_count
    col_of_owner = owner_block % tp_count
    first_range = band_of_owner * block_size // rows_dev
    offsets = jnp.arange(depth, dtype=jnp.int32)
    source_range = jnp.minimum(first_range[None, :] + offsets[:, None], fsdp_count - 1)
    source = source_range * tp_count + col_of_owner[None, :]
    outgoing = spread[source]
    landed = lax.all_to_all(outgoing, ("fsdp", "tp"), split_axis=1, concat_axis=1, tiled=True)
    column = landed.reshape(depth * rows_dev, block_size)
    start_row = band_of_owner[self_id] * block_size - first_range[self_id] * rows_dev
    own_block = lax.dynamic_slice_in_dim(column, start_row, block_size, 0)
    held = own_block * owner_count[self_id].astype(jnp.bfloat16)
    gram_left = lax.dot_general(
        held, held, (((1,), (1,)), ((), ())), preferred_element_type=jnp.float32
    )
    gram_right = lax.dot_general(
        held, held, (((0,), (0,)), ((), ())), preferred_element_type=jnp.float32
    )
    new_left = left_stat[0] + gram_left
    new_right = right_stat[0] + gram_right
    mixed_rows = jnp.dot(left_root[0], own_block, preferred_element_type=jnp.float32).astype(
        jnp.bfloat16
    )
    finished = jnp.dot(mixed_rows, right_root[0], preferred_element_type=jnp.float32).astype(
        jnp.bfloat16
    )
    placed = lax.dynamic_update_slice_in_dim(
        jnp.zeros((depth * rows_dev, block_size), jnp.bfloat16), finished, start_row, 0
    )
    placed = placed.reshape(depth, owners, sub_pieces, lane_width)
    returned = lax.all_to_all(placed, ("fsdp", "tp"), split_axis=1, concat_axis=1, tiled=True)
    source_ids = jnp.arange(owners, dtype=jnp.int32)
    source_fsdp = source_ids // tp_count
    source_col = source_ids % tp_count
    piece_steps = jnp.arange(sub_pieces, dtype=jnp.int32)
    local_rows = (self_id * sub_pieces + piece_steps) * lane_width // block_size
    global_rows = source_fsdp[:, None] * rows_dev + local_rows[None, :]
    band_rows = global_rows // block_size
    holder = block_owner[band_rows * tp_count + source_col[:, None]]
    range_step = source_fsdp[:, None] - band_rows * block_size // rows_dev
    piece_grid = jnp.broadcast_to(piece_steps[None, :], (owners, sub_pieces))
    picked = returned[range_step, holder, piece_grid]
    restored = lax.all_to_all(picked, ("fsdp", "tp"), split_axis=0, concat_axis=0, tiled=True)
    result = restored.reshape(rows_dev, block_size)
    return (new_left[None], new_right[None], result)


def solution(mesh):
    placed = (
        P("fsdp", "tp"),
        P(("fsdp", "tp"), None, None),
        P(("fsdp", "tp"), None, None),
        P(("fsdp", "tp"), None, None),
        P(("fsdp", "tp"), None, None),
        P(),
        P(),
        P(),
    )
    return jax.shard_map(
        body,
        mesh=mesh,
        in_specs=placed,
        out_specs=(P(("fsdp", "tp"), None, None), P(("fsdp", "tp"), None, None), P("fsdp", "tp")),
        check_vma=False,
    )
```

profile of v0, /device:TPU:1, one launch (start us, length us, event | category | flops | bytes accessed | tf_op | source)
XLA Modules:
  0.0 243.7 jit_solution(9753622686275061019)
XLA Ops:
  0.6 0.0 copy-start
  0.7 2.3 reshape.381
  3.0 11.5 %all-to-all-start = ((bf16[128,24,128]{2,1,0:T(8,128)(2,1)}), bf16[128,24,128]{2,1,0:T(8,128)(2,1)S(1)}, u32[]{:S(2)}, u32[]{:S(2)}) async-start(bf16[128,24,128]{2,1,0:T(8,128)(2,1)} %reshape.381), calls=%async_computation | async-start | bytes 1572864 | tf_op jit(solution)/shard_map/all_to_all | solution.py:19
  14.5 16.4 %all-to-all-done = bf16[128,24,128]{2,1,0:T(8,128)(2,1)S(1)} async-done(((bf16[128,24,128]{2,1,0:T(8,128)(2,1)}), bf16[128,24,128]{2,1,0:T(8,128)(2,1)S(1)}, u32[]{:S(2)}, u32[]{:S(2)}) %all-to-all-start) | async-done | bytes 786464 | tf_op jit(solution)/shard_map/all_to_all | solution.py:19
  30.9 3.2 %gather_fusion = bf16[512,24,128]{2,1,0:T(8,128)(2,1)} fusion(bf16[128,24,128]{2,1,0:T(8,128)(2,1)S(1)} %all-to-all-done, s32[1024]{0:T(1024)S(1)} %pad_clamp_fusion), kind=kCustom, calls=%fused_computation | custom fusion | bytes 6293504 | tf_op jit(solution)/shard_map/gather | solution.py:32
  34.1 4.1 %copy.12 = bf16[4,128,24,128]{3,2,0,1:T(8,128)(2,1)} copy(bf16[4,128,24,128]{3,2,1,0:T(8,128)(2,1)} %bitcast.36) | data formatting | bytes 6291456 | tf_op jit(solution)/shard_map/gather | solution.py:32
  38.2 5.4 %all-to-all-start.1 = ((bf16[4,128,24,128]{3,2,0,1:T(8,128)(2,1)}), bf16[4,128,24,128]{3,2,0,1:T(8,128)(2,1)}, u32[]{:S(2)}, u32[]{:S(2)}) async-start(bf16[4,128,24,128]{3,2,0,1:T(8,128)(2,1)} %copy.12), calls=%async_computation.1 | async-start | bytes 6291456 | tf_op jit(solution)/shard_map/all_to_all | solution.py:33
  43.6 0.6 dynamic_slice.13
  44.2 0.6 dynamic_slice.12
  46.1 38.2 %all-to-all-done.1 = bf16[4,128,24,128]{3,2,0,1:T(8,128)(2,1)} async-done(((bf16[4,128,24,128]{3,2,0,1:T(8,128)(2,1)}), bf16[4,128,24,128]{3,2,0,1:T(8,128)(2,1)}, u32[]{:S(2)}, u32[]{:S(2)}) %all-to-all-start.1) | async-done | bytes 3145760 | tf_op jit(solution)/shard_map/all_to_all | solution.py:33
  84.3 4.1 %copy.13 = bf16[4,128,24,128]{3,2,1,0:T(8,128)(2,1)} copy(bf16[4,128,24,128]{3,2,0,1:T(8,128)(2,1)} %all-to-all-done.1) | data formatting | bytes 6291456 | tf_op jit(solution)/shard_map/all_to_all | solution.py:33
  88.4 5.8 %reshape.382 = bf16[1536,1024]{1,0:T(8,128)(2,1)} reshape(bf16[4,128,24,128]{3,2,1,0:T(8,128)(2,1)} %copy.13) | data formatting | bytes 6291456 | tf_op jit(solution)/shard_map/reshape | solution.py:34
  94.2 2.1 broadcast_in_dim.10
  96.2 8.1 %convert_dynamic-update-slice_fusion = bf16[1536,1024]{1,0:T(8,128)(2,1)} fusion(bf16[1536,1024]{1,0:T(8,128)(2,1)} %broadcast_in_dim.10, s32[]{:T(128)S(6)} %select_n.126, bf16[1,1024,1024]{2,1,0:T(8,128)(2,1)S(1)} %copy-done, bf16[1,1024,1024]{2,1,0:T(8,128)(2,1)} %param.11, bf16[1536,1024]{1,0:T(8,128)(2,1)} %reshape.382), kind=kOutput, calls=%fused_computation.11 | convolution fusion | flops 4297064448 | bytes 8389632 | tf_op jit(solution)/shard_map/dot_general | solution.py:49
  104.3 5.8 %reshape.383 = bf16[4,128,24,128]{3,2,1,0:T(8,128)(2,1)} reshape(bf16[1536,1024]{1,0:T(8,128)(2,1)} %convert_dynamic-update-slice_fusion) | data formatting | bytes 6291456 | tf_op jit(solution)/shard_map/reshape | solution.py:55
  110.2 4.1 %copy.14 = bf16[4,128,24,128]{3,2,0,1:T(8,128)(2,1)} copy(bf16[4,128,24,128]{3,2,1,0:T(8,128)(2,1)} %reshape.383) | data formatting | bytes 6291456 | tf_op jit(solution)/shard_map/reshape | solution.py:55
  114.3 5.9 %all-to-all-start.2 = ((bf16[4,128,24,128]{3,2,0,1:T(8,128)(2,1)}), bf16[4,128,24,128]{3,2,0,1:T(8,128)(2,1)}, u32[]{:S(2)}, u32[]{:S(2)}) async-start(bf16[4,128,24,128]{3,2,0,1:T(8,128)(2,1)} %copy.14), calls=%async_computation.2 | async-start | bytes 6291456 | tf_op jit(solution)/shard_map/all_to_all | solution.py:56
  120.2 0.6 dynamic_slice.15
  121.5 0.1 compare_select_fusion.1
  121.6 0.1 reshape.395
  121.7 18.7 %gather_fusion.1 = s32[3072]{0:T(1024)S(1)} fusion(s32[48]{0:T(128)S(1)} %copy-done.1, s32[3072]{0:T(1024)S(1)} %broadcast_clamp_fusion), kind=kCustom, calls=%fused_computation.1 | custom fusion | bytes 36864 | tf_op jit(solution)/shard_map/gather | solution.py:64
  140.4 0.1 gather.13
  140.5 0.2 fusion.34
  140.7 0.1 reshape.401
  140.8 20.1 %all-to-all-done.2 = bf16[4,128,24,128]{3,2,0,1:T(8,128)(2,1)} async-done(((bf16[4,128,24,128]{3,2,0,1:T(8,128)(2,1)}), bf16[4,128,24,128]{3,2,0,1:T(8,128)(2,1)}, u32[]{:S(2)}, u32[]{:S(2)}) %all-to-all-start.2) | async-done | bytes 3145760 | tf_op jit(solution)/shard_map/all_to_all | solution.py:56
  160.9 4.1 %copy.15 = bf16[4,128,24,128]{3,2,1,0:T(8,128)(2,1)} copy(bf16[4,128,24,128]{3,2,0,1:T(8,128)(2,1)} %all-to-all-done.2) | data formatting | bytes 6291456 | tf_op jit(solution)/shard_map/all_to_all | solution.py:56
  165.0 56.1 %gather_fusion.2 = bf16[3072,128]{1,0:T(8,128)(2,1)} fusion(bf16[4,128,24,128]{3,2,1,0:T(8,128)(2,1)} %copy.15, s32[3072]{0:T(1024)S(1)} %reshape.401), kind=kCustom, calls=%fused_computation.2 | custom fusion | bytes 1609728 | tf_op jit(solution)/shard_map/gather | solution.py:67
  221.1 4.9 %all-to-all-start.3 = ((bf16[128,24,128]{2,1,0:T(8,128)(2,1)}), bf16[128,24,128]{2,1,0:T(8,128)(2,1)S(1)}, u32[]{:S(2)}, u32[]{:S(2)}) async-start(bf16[128,24,128]{2,1,0:T(8,128)(2,1)} %bitcast.10), calls=%async_computation.3 | async-start | bytes 1572864 | tf_op jit(solution)/shard_map/all_to_all | solution.py:68
  226.1 8.0 %fusion = f32[1,1024,1024]{2,1,0:T(8,128)} fusion(f32[1,1024,1024]{2,1,0:T(8,128)} %param.10, bf16[1536,1024]{1,0:T(8,128)(2,1)} %reshape.382, s32[]{:T(128)S(6)} %select_n.126, bf16[]{:T(256)} %bitcast.4), kind=kOutput, calls=%fused_computation.4 | convolution fusion | flops 2152726528 | bytes 10486276 | tf_op jit(solution)/shard_map/dot_general | solution.py:41
  234.1 4.4 %fusion.1 = f32[1,1024,1024]{2,1,0:T(8,128)} fusion(f32[1,1024,1024]{2,1,0:T(8,128)S(1)} %copy-done.4, bf16[1536,1024]{1,0:T(8,128)(2,1)S(1)} %copy-done.2, s32[]{:T(128)S(6)} %select_n.126, bf16[]{:T(256)} %bitcast.4), kind=kOutput, calls=%fused_computation.6 | convolution fusion | flops 2152726528 | bytes 10485766 | tf_op jit(solution)/shard_map/dot_general | solution.py:38
  238.5 4.0 %all-to-all-done.3 = bf16[128,24,128]{2,1,0:T(8,128)(2,1)S(1)} async-done(((bf16[128,24,128]{2,1,0:T(8,128)(2,1)}), bf16[128,24,128]{2,1,0:T(8,128)(2,1)S(1)}, u32[]{:S(2)}, u32[]{:S(2)}) %all-to-all-start.3) | async-done | bytes 786464 | tf_op jit(solution)/shard_map/all_to_all | solution.py:68
  242.5 1.2 reshape.384
  (17 shorter events, 0.1 us)
Async XLA Ops:
  0.6 95.6 %copy-start = (bf16[1,1024,1024]{2,1,0:T(8,128)(2,1)S(1)}, bf16[1,1024,1024]{2,1,0:T(8,128)(2,1)}, u32[]{:S(2)}) copy-start(bf16[1,1024,1024]{2,1,0:T(8,128)(2,1)} %param.12) | copy-start | bytes 6291460
  0.6 13.8 %copy-start.3 = (s32[128]{0:T(128)S(1)}, s32[128]{0:T(128)}, u32[]{:S(2)}) copy-start(s32[128]{0:T(128)} %param.14) | copy-start | bytes 1540
  3.0 28.0 %all-to-all-start = ((bf16[128,24,128]{2,1,0:T(8,128)(2,1)}), bf16[128,24,128]{2,1,0:T(8,128)(2,1)S(1)}, u32[]{:S(2)}, u32[]{:S(2)}) async-start(bf16[128,24,128]{2,1,0:T(8,128)(2,1)} %reshape.381), calls=%async_computation | async-start | bytes 1572864 | tf_op jit(solution)/shard_map/all_to_all | solution.py:19
  38.2 46.1 %all-to-all-start.1 = ((bf16[4,128,24,128]{3,2,0,1:T(8,128)(2,1)}), bf16[4,128,24,128]{3,2,0,1:T(8,128)(2,1)}, u32[]{:S(2)}, u32[]{:S(2)}) async-start(bf16[4,128,24,128]{3,2,0,1:T(8,128)(2,1)} %copy.12), calls=%async_computation.1 | async-start | bytes 6291456 | tf_op jit(solution)/shard_map/all_to_all | solution.py:33
  114.3 5.9 %copy-start.5 = (s32[128]{0:T(128)S(1)}, s32[128]{0:T(128)}, u32[]{:S(2)}) copy-start(s32[128]{0:T(128)} %param.15) | copy-start | bytes 1540
  114.3 7.4 %copy-start.1 = (s32[48]{0:T(128)S(1)}, s32[48]{0:T(128)}, u32[]{:S(2)}) copy-start(s32[48]{0:T(128)} %param.13) | copy-start | bytes 580
  114.3 46.6 %all-to-all-start.2 = ((bf16[4,128,24,128]{3,2,0,1:T(8,128)(2,1)}), bf16[4,128,24,128]{3,2,0,1:T(8,128)(2,1)}, u32[]{:S(2)}, u32[]{:S(2)}) async-start(bf16[4,128,24,128]{3,2,0,1:T(8,128)(2,1)} %copy.14), calls=%async_computation.2 | async-start | bytes 6291456 | tf_op jit(solution)/shard_map/all_to_all | solution.py:56
  221.1 21.4 %all-to-all-start.3 = ((bf16[128,24,128]{2,1,0:T(8,128)(2,1)}), bf16[128,24,128]{2,1,0:T(8,128)(2,1)S(1)}, u32[]{:S(2)}, u32[]{:S(2)}) async-start(bf16[128,24,128]{2,1,0:T(8,128)(2,1)} %bitcast.10), calls=%async_computation.3 | async-start | bytes 1572864 | tf_op jit(solution)/shard_map/all_to_all | solution.py:68
  226.0 8.0 %copy-start.2 = (bf16[1536,1024]{1,0:T(8,128)(2,1)S(1)}, bf16[1536,1024]{1,0:T(8,128)(2,1)}, u32[]{:S(2)}) copy-start(bf16[1536,1024]{1,0:T(8,128)(2,1)} %reshape.382) | copy-start | bytes 9437188
  226.1 8.0 %copy-start.4 = (f32[1,1024,1024]{2,1,0:T(8,128)S(1)}, f32[1,1024,1024]{2,1,0:T(8,128)}, u32[]{:S(2)}) copy-start(f32[1,1024,1024]{2,1,0:T(8,128)} %param.9) | copy-start | bytes 12582916
where the time goes:
time: 245 us; the launch traced here: 244 us
  local copies, waits for them, and re-layouts  114 us (47%)
  waiting for transfers between devices  78.8 us (32%)
  starting transfers between devices  27.7 us (11%)
  matrix products  20.5 us (8%)
  between operations  2.76 us (1%)
    gather x1, local copies, waits for them, and re-layouts, body(): picked = returned[range_step, holder, piece_grid]  56.1 us
    all_to_all x1, waiting for transfers between devices, body(): lax.all_to_all(outgoing, ('fsdp', 'tp'), split_axis=1, concat_axis=1, til...  38.2 us
    all_to_all x1, waiting for transfers between devices, body(): lax.all_to_all(placed, ('fsdp', 'tp'), split_axis=1, concat_axis=1, tiled...  20.1 us
    gather x2, local copies, waits for them, and re-layouts, body(): holder = block_owner[band_rows * tp_count + source_col[:, None]]  18.7 us
    all_to_all x1, waiting for transfers between devices, body(): lax.all_to_all(grad.reshape(owners, sub_pieces, lane_width), ('fsdp', 'tp...  16.4 us
    all_to_all x1, starting transfers between devices, body(): lax.all_to_all(grad.reshape(owners, sub_pieces, lane_width), ('fsdp', 'tp...  11.5 us
    reshape x2, local copies, waits for them, and re-layouts, body(): placed = placed.reshape(depth, owners, sub_pieces, lane_width)  9.92 us
    dot_general x1, matrix products, body(): jnp.dot(mixed_rows, right_root[0], preferred_element_type=jnp.float32)  8.12 us
  transfers between devices with their start and end apart: 4, of which 4 were waited for; matrix products, arithmetic and copies ran while one was open for 14% of the time, Pallas kernels for 0%

commit v1 on v0

v1 whole, which is shorter than its diff:
```python
import jax
import jax.numpy as jnp
from jax import lax
from jax.experimental import pallas as pl
from jax.experimental.pallas import tpu as pltpu
from jax.sharding import PartitionSpec as P

MESH = pl.DeviceIdType.MESH
BS = 1024
FS = 8
TP = 16
NB = 48
OWNERS = FS * TP
CHUNK = BS // FS
RR, RC = 16, 512
PER = 3


def region_rows(chunk, t):
    return pl.ds(pl.multiple_of(chunk * CHUNK + (t // 2) * RR, RR), RR)


def region_cols(t):
    return pl.ds(pl.multiple_of((t % 2) * RC, RC), RC)


def swapped(k):
    return (k // 4) * 4 + 3 - k % 4


def shifted_t(t, n):
    return ((t // 4 + n // 4) % 4) * 4 + (t % 4 + n % 4) % 4


def shifted_f(f, n):
    return ((f // 2 + n // 2) % 4) * 2 + (f % 2 + n % 2) % 2


def wait_bytes(ref, sem):
    pltpu.make_async_copy(ref, ref, sem).wait()


def route_kernel(
    owner_block, block_owner, grad, left_root, right_root,
    held, update,
    inter, stage, mixed, done, ret, back,
    send_sem, recv_sem,
):
    f = lax.axis_index("fsdp")
    t = lax.axis_index("tp")
    me = f * TP + t
    my_chunk = swapped(f)

    barrier = pltpu.get_barrier_semaphore()

    @pl.loop(1, OWNERS)
    def _(n):
        o = (me + n) % OWNERS
        pl.semaphore_signal(barrier, inc=1, device_id=(o // TP, o % TP), device_id_type=MESH)

    pl.semaphore_wait(barrier, OWNERS - 1)

    @pl.loop(0, PER * TP)
    def _(n):
        q = n % PER
        chunk = f * PER + q
        to_t = shifted_t(t, n // PER)
        pltpu.make_async_remote_copy(
            src_ref=grad.at[region_rows(q, to_t), region_cols(to_t)],
            dst_ref=inter.at[(chunk // FS) * TP + t],
            send_sem=send_sem.at[0],
            recv_sem=recv_sem.at[0],
            device_id=(swapped(chunk % FS), to_t),
            device_id_type=MESH,
        ).start()

    wait_bytes(inter, recv_sem.at[0])

    stage[me] = inter[owner_block[me]]
    pltpu.make_async_copy(
        stage.at[me], held.at[region_rows(my_chunk, t), region_cols(t)], recv_sem.at[1]
    ).start()

    @pl.loop(1, OWNERS)
    def _(n):
        m = (n * 37) % OWNERS
        to_f = shifted_f(f, m // TP)
        to_t = shifted_t(t, m % TP)
        o = to_f * TP + to_t
        stage[o] = inter[owner_block[o]]
        pltpu.make_async_remote_copy(
            src_ref=stage.at[o],
            dst_ref=held.at[region_rows(my_chunk, t), region_cols(t)],
            send_sem=send_sem.at[1],
            recv_sem=recv_sem.at[1],
            device_id=(to_f, to_t),
            device_id_type=MESH,
        ).start()

    wait_bytes(held, recv_sem.at[1])

    @pl.loop(0, 4)
    def _(c):
        rows = pl.ds(pl.multiple_of(c * 256, 256), 256)
        mixed[rows, :] = jnp.dot(
            left_root[rows, :], held[...], preferred_element_type=jnp.float32
        ).astype(jnp.bfloat16)

    @pl.loop(0, 4)
    def _(c):
        rows = pl.ds(pl.multiple_of(c * 256, 256), 256)
        done[rows, :] = jnp.dot(
            mixed[rows, :], right_root[...], preferred_element_type=jnp.float32
        ).astype(jnp.bfloat16)

    pltpu.make_async_copy(
        done.at[region_rows(my_chunk, t), region_cols(t)], ret.at[me], recv_sem.at[2]
    ).start()

    @pl.loop(1, OWNERS)
    def _(n):
        m = (n * 37) % OWNERS
        to_f = shifted_f(f, m // TP)
        to_t = shifted_t(t, m % TP)
        pltpu.make_async_remote_copy(
            src_ref=done.at[region_rows(swapped(to_f), to_t), region_cols(to_t)],
            dst_ref=ret.at[me],
            send_sem=send_sem.at[2],
            recv_sem=recv_sem.at[2],
            device_id=(to_f, to_t),
            device_id_type=MESH,
        ).start()

    wait_bytes(ret, recv_sem.at[2])

    @pl.loop(0, NB)
    def _(n):
        band = n % PER
        to_t = shifted_t(t, n // PER)
        b = band * TP + to_t
        chunk = band * FS + my_chunk
        back[b] = ret[block_owner[b]]
        pltpu.make_async_remote_copy(
            src_ref=back.at[b],
            dst_ref=update.at[region_rows(chunk % PER, t), region_cols(t)],
            send_sem=send_sem.at[3],
            recv_sem=recv_sem.at[3],
            device_id=(chunk // PER, to_t),
            device_id_type=MESH,
        ).start()

    wait_bytes(inter, send_sem.at[0])
    wait_bytes(stage.at[pl.ds(0, OWNERS - 1)], send_sem.at[1])
    wait_bytes(ret.at[pl.ds(0, OWNERS - 1)], send_sem.at[2])
    wait_bytes(back, send_sem.at[3])
    wait_bytes(update, recv_sem.at[3])


def route(owner_block, block_owner, grad, left_root, right_root):
    vmem = pl.BlockSpec(memory_space=pltpu.VMEM)
    smem = pl.BlockSpec(memory_space=pltpu.SMEM)
    return pl.pallas_call(
        route_kernel,
        out_shape=(
            jax.ShapeDtypeStruct((BS, BS), jnp.bfloat16),
            jax.ShapeDtypeStruct(grad.shape, jnp.bfloat16),
        ),
        in_specs=[smem, smem, vmem, vmem, vmem],
        out_specs=(vmem, vmem),
        scratch_shapes=[
            pltpu.VMEM((NB, RR, RC), jnp.bfloat16),
            pltpu.VMEM((OWNERS, RR, RC), jnp.bfloat16),
            pltpu.VMEM((BS, BS), jnp.bfloat16),
            pltpu.VMEM((BS, BS), jnp.bfloat16),
            pltpu.VMEM((OWNERS, RR, RC), jnp.bfloat16),
            pltpu.VMEM((NB, RR, RC), jnp.bfloat16),
            pltpu.SemaphoreType.DMA((4,)),
            pltpu.SemaphoreType.DMA((4,)),
        ],
        compiler_params=pltpu.CompilerParams(
            collective_id=0, has_side_effects=True, vmem_limit_bytes=40 * 1024 * 1024
        ),
        cost_estimate=pl.CostEstimate(
            flops=4 * BS**3, bytes_accessed=12 * BS * BS, transcendentals=0
        ),
        name="route",
    )(owner_block, block_owner, grad, left_root, right_root)


def body(grad, left_stat, right_stat, left_root, right_root, block_owner, owner_block, owner_count):
    me = lax.axis_index("fsdp") * TP + lax.axis_index("tp")
    own_block, update = route(owner_block, block_owner, grad, left_root[0], right_root[0])
    held = own_block * owner_count[me].astype(jnp.bfloat16)
    gram_left = lax.dot_general(
        held, held, (((1,), (1,)), ((), ())), preferred_element_type=jnp.float32
    )
    gram_right = lax.dot_general(
        held, held, (((0,), (0,)), ((), ())), preferred_element_type=jnp.float32
    )
    return (left_stat[0] + gram_left)[None], (right_stat[0] + gram_right)[None], update


def solution(mesh):
    whole = P(("fsdp", "tp"), None, None)
    return jax.shard_map(
        body,
        mesh=mesh,
        in_specs=(P("fsdp", "tp"), whole, whole, whole, whole, P(), P(), P()),
        out_specs=(whole, whole, P("fsdp", "tp")),
        check_vma=False,
    )
```

time: 245 us -> 115 us (0.47)
  local copies, waits for them, and re-layouts: 114 us -> 7.75 us
  Pallas kernels: 0 us -> 96.7 us
  waiting for transfers between devices: 78.8 us -> 0 us
  starting transfers between devices: 27.7 us -> 0 us
  matrix products: 20.5 us -> 8.94 us
    pallas_call x0 -> x1, Pallas kernels: none -> 96.7 us  [route(): pl.pallas_call(route_kernel, out_shape=(jax.ShapeDtypeStruct((BS, BS), jn...]
    gather x5 -> x0, local copies, waits for them, and re-layouts: 82.1 us -> none  [the longest x1 56.1 us: body(): picked = returned[range_step, holder, piece_grid]]
    all_to_all x4 -> x0, waiting for transfers between devices: 78.8 us -> none  [the longest x1 38.2 us: body(): lax.all_to_all(outgoing, ('fsdp', 'tp'), split_axis=1, concat_axis=1, til...]
    all_to_all x4 -> x0, starting transfers between devices: 27.7 us -> none  [the longest x1 11.5 us: body(): lax.all_to_all(grad.reshape(owners, sub_pieces, lane_width), ('fsdp', 'tp...]
    reshape x5 -> x0, local copies, waits for them, and re-layouts: 19.2 us -> none  [the longest x2 9.92 us: body(): placed = placed.reshape(depth, owners, sub_pieces, lane_width)]
    all_to_all x2 -> x0, local copies, waits for them, and re-layouts: 8.18 us -> none  [the longest x1 4.09 us: body(): lax.all_to_all(outgoing, ('fsdp', 'tp'), split_axis=1, concat_axis=1, til...]
    dot_general x1 -> x0, matrix products: 8.12 us -> none  [body(): jnp.dot(mixed_rows, right_root[0], preferred_element_type=jnp.float32)]
    unnamed x12 -> x15, local copies, waits for them, and re-layouts: 0.03 us -> 6.51 us
  transfers between devices with their start and end apart: 4 -> 0, of which waited for: 4 -> 0; matrix products, arithmetic and copies ran while one was open for 14% -> 0% of each run, Pallas kernels for 0% -> 0%
where the time goes in v1:
time: 115 us
  Pallas kernels  96.7 us (84%)
  matrix products  8.94 us (8%)
  local copies, waits for them, and re-layouts  7.75 us (7%)
  between operations  1.33 us (1%)
    pallas_call x1, Pallas kernels, route(): pl.pallas_call(route_kernel, out_shape=(jax.ShapeDtypeStruct((BS, BS), jn...  96.7 us
    unnamed x15, local copies, waits for them, and re-layouts  6.51 us
    dot_general x1, matrix products, body(): lax.dot_general(held, held, (((0,), (0,)), ((), ())), preferred_element_t...  4.54 us
    dot_general x1, matrix products, body(): lax.dot_general(held, held, (((1,), (1,)), ((), ())), preferred_element_t...  4.39 us

profile of v1, /device:TPU:1, one launch (start us, length us, event | category | flops | bytes accessed | tf_op | source)
XLA Modules:
  0.0 114.7 jit_solution(15349896129854355633)
XLA Ops:
  0.6 1.2 %dynamic_slice.3 = s32[1]{0:T(128)} dynamic-slice(s32[128]{0:T(128)} %param.15, s32[]{:T(128)S(6)} %select_n.3), dynamic_slice_sizes={1} | dynamic-slice | bytes 12 | tf_op jit(solution)/shard_map/dynamic_slice | solution.py:193
  2.5 0.0 copy-start
  2.5 1.6 %copy-done = bf16[1,1024,1024]{2,1,0:T(8,128)(2,1)S(1)} copy-done((bf16[1,1024,1024]{2,1,0:T(8,128)(2,1)S(1)}, bf16[1,1024,1024]{2,1,0:T(8,128)(2,1)}, u32[]{:S(2)}) %copy-start) | copy-done | bytes 2097176
  4.1 0.0 copy-start.1
  4.1 1.6 %copy-done.1 = bf16[1,1024,1024]{2,1,0:T(8,128)(2,1)S(1)} copy-done((bf16[1,1024,1024]{2,1,0:T(8,128)(2,1)S(1)}, bf16[1,1024,1024]{2,1,0:T(8,128)(2,1)}, u32[]{:S(2)}) %copy-start.1) | copy-done | bytes 2097176
  5.7 0.0 copy-start.2
  5.7 1.1 copy-done.2
  6.9 0.0 copy-start.3
  6.9 0.7 copy-done.3
  7.5 0.0 copy-start.4
  7.5 0.7 copy-done.4
  8.2 0.0 copy-start.5
  8.2 96.7 %route.1 = (bf16[1024,1024]{1,0:T(8,128)(2,1)S(1)}, bf16[384,1024]{1,0:T(8,128)(2,1)S(1)}) custom-call(s32[128]{0:T(128)S(1)} %copy-done.3, s32[48]{0:T(128)S(1)} %copy-done.4, bf16[384,1024]{1,0:T(8,128)(2,1)S(1)} %copy-done.2, bf16[1024,1024]{1,0:T(8,128)(2,1)S(1)} %bitcast.15, bf16[1024,1024]{1,0:T(8,128)(2,1)S(1)} %bitcast.16), custom_call_target="tpu_custom_call" | custom-call | flops 4294967296 | bytes 12582912 | tf_op jit(solution)/shard_map/route/pallas_call | solution.py:162
  104.9 0.0 copy-done.5
  104.9 0.0 copy-start.6
  104.9 4.5 %fusion = f32[1,1024,1024]{2,1,0:T(8,128)} fusion(f32[1,1024,1024]{2,1,0:T(8,128)S(1)} %copy-done.5, bf16[1024,1024]{1,0:T(8,128)(2,1)S(1)} %get-tuple-element.5, bf16[]{:T(256)} %bitcast.3), kind=kOutput, calls=%fused_computation.1 | convolution fusion | flops 2149580800 | bytes 10485762 | tf_op jit(solution)/shard_map/dot_general | solution.py:197
  109.4 0.0 copy-done.6
  109.4 4.4 %fusion.1 = f32[1,1024,1024]{2,1,0:T(8,128)} fusion(f32[1,1024,1024]{2,1,0:T(8,128)S(1)} %copy-done.6, bf16[1024,1024]{1,0:T(8,128)(2,1)S(1)} %get-tuple-element.5, bf16[]{:T(256)} %bitcast.3), kind=kOutput, calls=%fused_computation.3 | convolution fusion | flops 2149580800 | bytes 10485762 | tf_op jit(solution)/shard_map/dot_general | solution.py:194
  113.8 0.9 copy.12
Async XLA Ops:
  2.5 1.6 %copy-start = (bf16[1,1024,1024]{2,1,0:T(8,128)(2,1)S(1)}, bf16[1,1024,1024]{2,1,0:T(8,128)(2,1)}, u32[]{:S(2)}) copy-start(bf16[1,1024,1024]{2,1,0:T(8,128)(2,1)} %param.11) | copy-start | bytes 6291460
  4.1 1.6 %copy-start.1 = (bf16[1,1024,1024]{2,1,0:T(8,128)(2,1)S(1)}, bf16[1,1024,1024]{2,1,0:T(8,128)(2,1)}, u32[]{:S(2)}) copy-start(bf16[1,1024,1024]{2,1,0:T(8,128)(2,1)} %param.12) | copy-start | bytes 6291460
  5.7 1.1 copy-start.2
  6.9 0.7 copy-start.3
  7.5 0.7 copy-start.4
  8.2 96.7 %copy-start.5 = (f32[1,1024,1024]{2,1,0:T(8,128)S(1)}, f32[1,1024,1024]{2,1,0:T(8,128)}, u32[]{:S(2)}) copy-start(f32[1,1024,1024]{2,1,0:T(8,128)} %param.10) | copy-start | bytes 12582916
  104.9 4.6 %copy-start.6 = (f32[1,1024,1024]{2,1,0:T(8,128)S(1)}, f32[1,1024,1024]{2,1,0:T(8,128)}, u32[]{:S(2)}) copy-start(f32[1,1024,1024]{2,1,0:T(8,128)} %param.9) | copy-start | bytes 12582916

commit v2 on v1

v2 whole, which is shorter than its diff:
```python
import jax
import jax.numpy as jnp
from jax import lax
from jax.experimental import pallas as pl
from jax.experimental.pallas import tpu as pltpu
from jax.sharding import PartitionSpec as P

MESH = pl.DeviceIdType.MESH
BS = 1024
HALF = BS // 2
FS = 8
TP = 16
NB = 48
OWNERS = FS * TP
CHUNK = BS // FS
RR, RC = 16, 512
PER = 3
STEP = 256


def region_rows(chunk, t):
    return pl.ds(pl.multiple_of(chunk * CHUNK + (t // 2) * RR, RR), RR)


def region_cols(t):
    return pl.ds(pl.multiple_of((t % 2) * RC, RC), RC)


def chunk_to_f(k):
    return 2 * ((2 * (k % 4) + 1) % 5) + 1 - k // 4


def f_to_chunk(f):
    return (3 * (f // 2) + 2) % 5 + 4 * (1 - f % 2)


def shifted_t(t, n):
    return ((t // 4 + n // 4) % 4) * 4 + (t % 4 + n % 4) % 4


def wait_bytes(ref, sem):
    pltpu.make_async_copy(ref, ref, sem).wait()


def steps(first, last):
    def over(fn):
        @pl.loop(first // STEP, last // STEP)
        def _(c):
            fn(pl.ds(pl.multiple_of(c * STEP, STEP), STEP))

    return over


def route_kernel(
    owner_block_any, block_owner_any, owner_count_any, grad_any,
    left_root_any, right_root_any, left_stat_any, right_stat_any,
    new_left, new_right, update,
    owner_block, block_owner, owner_count, grad, left_root, right_root,
    inter, stage, held, total, mixed, done, ret, back,
    local_sem, send_sem, recv_sem, land_sem,
):
    f = lax.axis_index("fsdp")
    t = lax.axis_index("tp")
    me = f * TP + t
    x, core = f // 2, f % 2
    my_chunk = f_to_chunk(f)

    fetches = [
        pltpu.make_async_copy(src, dst, local_sem.at[i])
        for i, (src, dst) in enumerate((
            (owner_block_any, owner_block),
            (block_owner_any, block_owner),
            (owner_count_any, owner_count),
            (grad_any, grad),
            (left_root_any, left_root),
            (right_root_any, right_root),
            (left_stat_any, new_left),
            (right_stat_any, new_right),
        ))
    ]
    for fetch in fetches:
        fetch.start()

    barrier = pltpu.get_barrier_semaphore()

    @pl.loop(1, OWNERS)
    def _(n):
        o = (me + n) % OWNERS
        pl.semaphore_signal(barrier, inc=1, device_id=(o // TP, o % TP), device_id_type=MESH)

    for fetch in fetches[:4]:
        fetch.wait()
    pl.semaphore_wait(barrier, OWNERS - 1)

    for part in range(2):
        for q in range(PER):
            chunk = f * PER + q
            k = chunk % FS

            @pl.when(k // 4 == part)
            def _():
                @pl.loop(0, TP)
                def _(n):
                    to_t = shifted_t(t, n)
                    pltpu.make_async_remote_copy(
                        src_ref=grad.at[region_rows(q, to_t), region_cols(to_t)],
                        dst_ref=inter.at[(chunk // FS) * TP + t],
                        send_sem=send_sem.at[0],
                        recv_sem=recv_sem.at[0],
                        device_id=(chunk_to_f(k), to_t),
                        device_id_type=MESH,
                    ).start()

    wait_bytes(inter, recv_sem.at[0])

    stage[me] = inter[owner_block[me]]
    pltpu.make_async_copy(
        stage.at[me], held.at[region_rows(my_chunk, t), region_cols(t)], land_sem.at[1 - core]
    ).start()

    @pl.loop(1, OWNERS)
    def _(n):
        m = (n * 37) % OWNERS
        to_f = ((x + m // 32) % 4) * 2 + (core + m // 16) % 2
        to_t = shifted_t(t, m % TP)
        o = to_f * TP + to_t
        stage[o] = inter[owner_block[o]]
        pltpu.make_async_remote_copy(
            src_ref=stage.at[o],
            dst_ref=held.at[region_rows(my_chunk, t), region_cols(t)],
            send_sem=send_sem.at[1],
            recv_sem=land_sem.at[1 - core],
            device_id=(to_f, to_t),
            device_id_type=MESH,
        ).start()

    fetches[4].wait()
    fetches[5].wait()
    wait_bytes(held.at[pl.ds(0, HALF)], land_sem.at[0])

    @steps(0, BS)
    def _(rows):
        total[rows, :] = jnp.dot(
            left_root[rows, pl.ds(0, HALF)], held[pl.ds(0, HALF), :],
            preferred_element_type=jnp.float32,
        )

    wait_bytes(held.at[pl.ds(HALF, HALF)], land_sem.at[1])

    for part in range(2):
        @steps(part * HALF, (part + 1) * HALF)
        def _(rows):
            mixed[rows, :] = (
                total[rows, :]
                + jnp.dot(
                    left_root[rows, pl.ds(HALF, HALF)], held[pl.ds(HALF, HALF), :],
                    preferred_element_type=jnp.float32,
                )
            ).astype(jnp.bfloat16)
            done[rows, :] = jnp.dot(
                mixed[rows, :], right_root[...], preferred_element_type=jnp.float32
            ).astype(jnp.bfloat16)

        to_core = 1 - part

        @pl.when(core == to_core)
        def _():
            pltpu.make_async_copy(
                done.at[region_rows(my_chunk, t), region_cols(t)], ret.at[me], recv_sem.at[1]
            ).start()

        def send_back(n):
            to_f = ((x + n // TP) % 4) * 2 + to_core
            to_t = shifted_t(t, n % TP)
            pltpu.make_async_remote_copy(
                src_ref=done.at[region_rows(f_to_chunk(to_f), to_t), region_cols(to_t)],
                dst_ref=ret.at[me],
                send_sem=send_sem.at[2],
                recv_sem=recv_sem.at[1],
                device_id=(to_f, to_t),
                device_id_type=MESH,
            ).start()

        @pl.when(core != to_core)
        def _():
            send_back(0)

        @pl.loop(1, OWNERS // 2)
        def _(n):
            send_back((n * 37) % (OWNERS // 2))

    count = owner_count[me].astype(jnp.float32)
    fetches[7].wait()

    @steps(0, BS)
    def _(rows):
        new_right[rows, :] += count * lax.dot_general(
            held[:, rows], held[...], (((0,), (0,)), ((), ())),
            preferred_element_type=jnp.float32,
        )

    wait_bytes(ret, recv_sem.at[1])

    @pl.loop(0, NB)
    def _(n):
        band = n % PER
        to_t = shifted_t(t, n // PER)
        b = band * TP + to_t
        chunk = band * FS + my_chunk
        back[b] = ret[block_owner[b]]
        pltpu.make_async_remote_copy(
            src_ref=back.at[b],
            dst_ref=update.at[region_rows(chunk % PER, t), region_cols(t)],
            send_sem=send_sem.at[3],
            recv_sem=recv_sem.at[2],
            device_id=(chunk // PER, to_t),
            device_id_type=MESH,
        ).start()

    fetches[6].wait()

    @steps(0, BS)
    def _(rows):
        new_left[rows, :] += count * lax.dot_general(
            held[rows, :], held[...], (((1,), (1,)), ((), ())),
            preferred_element_type=jnp.float32,
        )

    wait_bytes(inter, send_sem.at[0])
    wait_bytes(stage.at[pl.ds(0, OWNERS - 1)], send_sem.at[1])
    wait_bytes(ret.at[pl.ds(0, OWNERS - 1)], send_sem.at[2])
    wait_bytes(back, send_sem.at[3])
    wait_bytes(update, recv_sem.at[2])


def route(*operands):
    grad = operands[3]
    vmem = pl.BlockSpec(memory_space=pltpu.VMEM)
    stat = pltpu.VMEM((BS, BS), jnp.float32)
    square = pltpu.VMEM((BS, BS), jnp.bfloat16)
    return pl.pallas_call(
        route_kernel,
        out_shape=(stat, stat, pltpu.VMEM(grad.shape, jnp.bfloat16)),
        in_specs=[pl.BlockSpec(memory_space=pltpu.HBM)] * 8,
        out_specs=(vmem,) * 3,
        scratch_shapes=[
            pltpu.SMEM((OWNERS,), jnp.int32),
            pltpu.SMEM((NB,), jnp.int32),
            pltpu.SMEM((OWNERS,), jnp.int32),
            pltpu.VMEM(grad.shape, jnp.bfloat16),
            square,
            square,
            pltpu.VMEM((NB, RR, RC), jnp.bfloat16),
            pltpu.VMEM((OWNERS, RR, RC), jnp.bfloat16),
            square,
            pltpu.VMEM((BS, BS), jnp.float32),
            square,
            square,
            pltpu.VMEM((OWNERS, RR, RC), jnp.bfloat16),
            pltpu.VMEM((NB, RR, RC), jnp.bfloat16),
            pltpu.SemaphoreType.DMA((8,)),
            pltpu.SemaphoreType.DMA((4,)),
            pltpu.SemaphoreType.DMA((3,)),
            pltpu.SemaphoreType.DMA((2,)),
        ],
        compiler_params=pltpu.CompilerParams(
            collective_id=0, has_side_effects=True, vmem_limit_bytes=40 * 1024 * 1024
        ),
        cost_estimate=pl.CostEstimate(
            flops=8 * BS**3, bytes_accessed=24 * BS * BS, transcendentals=0
        ),
        name="route",
    )(*(pltpu.with_memory_space_constraint(a, pltpu.HBM) for a in operands))


def write_kernel(left, right, update, left_out, right_out, update_out, sems):
    copies = []
    for src, dst, parts in ((left, left_out, 4), (right, right_out, 4), (update, update_out, 1)):
        rows = src.shape[0] // parts
        for i in range(parts):
            piece = pl.ds(i * rows, rows)
            copies.append(pltpu.make_async_copy(src.at[piece], dst.at[piece], sems.at[len(copies)]))
    for copy in copies:
        copy.start()
    for copy in copies:
        copy.wait()


def write(*arrays):
    return pl.pallas_call(
        write_kernel,
        out_shape=tuple(jax.ShapeDtypeStruct(a.shape, a.dtype) for a in arrays),
        in_specs=[pl.BlockSpec(memory_space=pltpu.VMEM)] * 3,
        out_specs=(pl.BlockSpec(memory_space=pltpu.HBM),) * 3,
        scratch_shapes=[pltpu.SemaphoreType.DMA((9,))],
        compiler_params=pltpu.CompilerParams(vmem_limit_bytes=1024 * 1024),
        cost_estimate=pl.CostEstimate(flops=0, bytes_accessed=18 * BS * BS, transcendentals=0),
        name="write",
    )(*(pltpu.with_memory_space_constraint(a, pltpu.VMEM) for a in arrays))


def body(grad, left_stat, right_stat, left_root, right_root, block_owner, owner_block, owner_count):
    new_left, new_right, update = write(*route(
        owner_block, block_owner, owner_count, grad,
        left_root[0], right_root[0], left_stat[0], right_stat[0],
    ))
    return new_left[None], new_right[None], update


def solution(mesh):
    whole = P(("fsdp", "tp"), None, None)
    return jax.shard_map(
        body,
        mesh=mesh,
        in_specs=(P("fsdp", "tp"), whole, whole, whole, whole, P(), P(), P()),
        out_specs=(whole, whole, P("fsdp", "tp")),
        check_vma=False,
    )
```

time: 115 us -> 96 us (0.83)
  matrix products: 8.94 us -> 0 us
  local copies, waits for them, and re-layouts: 7.75 us -> 0 us
  Pallas kernels: 96.7 us -> 95.3 us
    dot_general x2 -> x0, matrix products: 8.94 us -> none  [the longest x1 4.54 us: body(): lax.dot_general(held, held, (((0,), (0,)), ((), ())), preferred_element_t...]
    unnamed x15 -> x0, local copies, waits for them, and re-layouts: 6.51 us -> none
    pallas_call x1 -> x2, Pallas kernels: 96.7 us -> 95.3 us  [the longest x1 91.7 us: route(): pl.pallas_call(route_kernel, out_shape=(stat, stat, pltpu.VMEM(grad.shape...]
    dynamic_slice x1 -> x0, local copies, waits for them, and re-layouts: 1.24 us -> none  [body(): held = own_block * owner_count[me].astype(jnp.bfloat16)]
where the time goes in v2:
time: 96 us; the launch traced here: 95.9 us
  Pallas kernels  95.3 us (99%)
    pallas_call x1, Pallas kernels, route(): pl.pallas_call(route_kernel, out_shape=(stat, stat, pltpu.VMEM(grad.shape...  91.7 us
    pallas_call x1, Pallas kernels, write(): pl.pallas_call(write_kernel, out_shape=tuple((jax.ShapeDtypeStruct(a.shap...  3.6 us

profile of v2, /device:TPU:1, one launch (start us, length us, event | category | flops | bytes accessed | tf_op | source)
XLA Modules:
  0.0 95.9 jit_solution(5846759808285996375)
XLA Ops:
  0.6 91.7 %route.1 = (f32[1024,1024]{1,0:T(8,128)S(1)}, f32[1024,1024]{1,0:T(8,128)S(1)}, bf16[384,1024]{1,0:T(8,128)(2,1)S(1)}) custom-call(s32[128]{0:T(128)} %owner_block_any.1, s32[48]{0:T(128)} %block_owner_any.1, s32[128]{0:T(128)} %owner_count_any.1, bf16[384,1024]{1,0:T(8,128)(2,1)} %grad_any.1, bf16[1024,1024]{1,0:T(8,128)(2,1)} %bitcast.10, ...), custom_call_target="tpu_custom_call" | custom-call | flops 8589934592 | bytes 25165824 | tf_op jit(solution)/shard_map/route/pallas_call | solution.py:241
  92.3 3.6 %write.1 = (f32[1024,1024]{1,0:T(8,128)}, f32[1024,1024]{1,0:T(8,128)}, bf16[384,1024]{1,0:T(8,128)(2,1)}) custom-call(f32[1024,1024]{1,0:T(8,128)S(1)} %get-tuple-element.9.left, f32[1024,1024]{1,0:T(8,128)S(1)} %get-tuple-element.10.right, bf16[384,1024]{1,0:T(8,128)(2,1)S(1)} %get-tuple-element.11.update), custom_call_target="tpu_custom_call" | custom-call | bytes 18874368 | tf_op jit(solution)/shard_map/write/pallas_call | solution.py:290

commit v3 on v2

v3 whole, which is shorter than its diff:
```python
import jax
import jax.numpy as jnp
from jax import lax
from jax.experimental import pallas as pl
from jax.experimental.pallas import tpu as pltpu
from jax.sharding import PartitionSpec as P

MESH = pl.DeviceIdType.MESH
BS = 1024
HALF = BS // 2
FS = 8
TP = 16
NB = 48
OWNERS = FS * TP
CHUNK = BS // FS
RR, RC = 16, 256
PER = 3
STEP = 256


def piece(chunk, half, t):
    return (
        pl.ds(pl.multiple_of(chunk * CHUNK + (t // 2) * RR, RR), RR),
        pl.ds(pl.multiple_of(half * HALF + (t % 2) * RC, RC), RC),
    )


def swapped(k):
    return (k // 4) * 4 + 3 - k % 4


def shifted_t(t, n):
    return ((t // 4 + n // 4) % 4) * 4 + (t % 4 + n % 4) % 4


def wait_bytes(ref, sem):
    pltpu.make_async_copy(ref, ref, sem).wait()


def steps(first, last):
    def over(fn):
        @pl.loop(first // STEP, last // STEP)
        def _(c):
            fn(pl.ds(pl.multiple_of(c * STEP, STEP), STEP))

    return over


def route_kernel(
    owner_block_any, block_owner_any, owner_count_any, grad_any,
    left_root_any, right_root_any, left_stat_any, right_stat_any,
    new_left, new_right, update,
    owner_block, block_owner, owner_count, grad, left_root, right_root,
    inter_0, inter_1, stage, held, total, mixed, done, ret_0, ret_1, back,
    local_sem, send_sem, recv_sem, heard_sem,
):
    f = lax.axis_index("fsdp")
    t = lax.axis_index("tp")
    me = f * TP + t
    x, core = f // 2, f % 2
    my_chunk = swapped(f)
    inter, ret = (inter_0, inter_1), (ret_0, ret_1)
    halves = [pl.ds(h * HALF, HALF) for h in range(2)]

    fetches = [
        pltpu.make_async_copy(src, dst, local_sem.at[i])
        for i, (src, dst) in enumerate((
            (owner_block_any, owner_block),
            (block_owner_any, block_owner),
            (owner_count_any, owner_count),
            (grad_any, grad),
            (left_root_any, left_root),
            (right_root_any, right_root),
            (left_stat_any, new_left),
            (right_stat_any, new_right),
        ))
    ]
    for fetch in fetches[:4]:
        fetch.start()

    targets = [swapped((f * PER + q) % FS) for q in range(PER)]
    sources = [(band * FS + my_chunk) // PER for band in range(PER)]
    barrier = pltpu.get_barrier_semaphore()

    for band in range(PER):
        for n in range(TP):
            pl.semaphore_signal(
                barrier, inc=1, device_id=(sources[band], (t + n) % TP), device_id_type=MESH
            )

    for fetch in fetches[:4]:
        fetch.wait()
    pl.semaphore_wait(barrier, PER * TP)

    def tell_targets(sem):
        for to_f in targets:
            pl.semaphore_signal(sem, inc=1, device_id=(to_f, t), device_id_type=MESH)

    tell_targets(heard_sem.at[0])

    for h in range(2):
        @pl.loop(0, PER * TP)
        def _(n):
            q = n % PER
            chunk = f * PER + q
            to_t = shifted_t(t, (n // PER) * 5 % TP)
            pltpu.make_async_remote_copy(
                src_ref=grad.at[piece(q, h, to_t)],
                dst_ref=inter[h].at[(chunk // FS) * TP + t],
                send_sem=send_sem.at[0, h],
                recv_sem=recv_sem.at[0, h],
                device_id=(swapped(chunk % FS), to_t),
                device_id_type=MESH,
            ).start()

    for fetch in fetches[4:]:
        fetch.start()

    pl.semaphore_wait(heard_sem.at[0], PER)
    tell_targets(heard_sem.at[1])

    for h in range(2):
        wait_bytes(inter[h], recv_sem.at[0, h])
        if h == 0:
            pl.semaphore_wait(heard_sem.at[1], PER)
        stage[h, me] = inter[h][owner_block[me]]
        pltpu.make_async_copy(
            stage.at[h, me], held.at[piece(my_chunk, h, t)], recv_sem.at[1, h]
        ).start()

        @pl.loop(1, OWNERS)
        def _(n):
            m = (n * 37) % OWNERS
            to_f = ((x + m // 32) % 4) * 2 + (core + m // 16) % 2
            to_t = shifted_t(t, m % TP)
            o = to_f * TP + to_t
            stage[h, o] = inter[h][owner_block[o]]
            pltpu.make_async_remote_copy(
                src_ref=stage.at[h, o],
                dst_ref=held.at[piece(my_chunk, h, t)],
                send_sem=send_sem.at[1, h],
                recv_sem=recv_sem.at[1, h],
                device_id=(to_f, to_t),
                device_id_type=MESH,
            ).start()

    fetches[4].wait()
    fetches[5].wait()

    def mix(h):
        @steps(h * HALF, (h + 1) * HALF)
        def _(cols):
            mixed[:, cols] = jnp.dot(
                left_root[...], held[:, cols], preferred_element_type=jnp.float32
            ).astype(jnp.bfloat16)

    def finish(h, cols):
        return jnp.dot(
            mixed[:, halves[h]], right_root[halves[h], cols], preferred_element_type=jnp.float32
        )

    wait_bytes(held.at[:, halves[0]], recv_sem.at[1, 0])
    mix(0)

    @steps(0, BS)
    def _(cols):
        total[:, cols] = finish(0, cols)

    wait_bytes(held.at[:, halves[1]], recv_sem.at[1, 1])
    mix(1)

    for h in range(2):
        @steps(h * HALF, (h + 1) * HALF)
        def _(cols):
            done[:, cols] = (total[:, cols] + finish(1, cols)).astype(jnp.bfloat16)

        pltpu.make_async_copy(
            done.at[piece(my_chunk, h, t)], ret[h].at[me], recv_sem.at[2, h]
        ).start()

        @pl.loop(1, OWNERS)
        def _(n):
            m = (n * 37) % OWNERS
            to_f = ((x + m // 32) % 4) * 2 + (core + m // 16) % 2
            to_t = shifted_t(t, m % TP)
            pltpu.make_async_remote_copy(
                src_ref=done.at[piece(swapped(to_f), h, to_t)],
                dst_ref=ret[h].at[me],
                send_sem=send_sem.at[2, h],
                recv_sem=recv_sem.at[2, h],
                device_id=(to_f, to_t),
                device_id_type=MESH,
            ).start()

    count = owner_count[me].astype(jnp.float32)

    def add_right():
        fetches[7].wait()

        @steps(0, BS)
        def _(rows):
            new_right[rows, :] += count * lax.dot_general(
                held[:, rows], held[...], (((0,), (0,)), ((), ())),
                preferred_element_type=jnp.float32,
            )

    def add_left():
        fetches[6].wait()

        @steps(0, BS)
        def _(rows):
            new_left[rows, :] += count * lax.dot_general(
                held[rows, :], held[...], (((1,), (1,)), ((), ())),
                preferred_element_type=jnp.float32,
            )

    for h in range(2):
        if h == 0:
            add_right()
        else:
            add_left()
        wait_bytes(ret[h], recv_sem.at[2, h])

        @pl.loop(0, NB)
        def _(n):
            band = n % PER
            to_t = shifted_t(t, (n // PER) * 5 % TP)
            b = band * TP + to_t
            chunk = band * FS + my_chunk
            back[h, b] = ret[h][block_owner[b]]
            pltpu.make_async_remote_copy(
                src_ref=back.at[h, b],
                dst_ref=update.at[piece(chunk % PER, h, t)],
                send_sem=send_sem.at[3, h],
                recv_sem=recv_sem.at[3, h],
                device_id=(chunk // PER, to_t),
                device_id_type=MESH,
            ).start()

    others = pl.ds(0, OWNERS - 1)
    for h in range(2):
        wait_bytes(inter[h], send_sem.at[0, h])
        wait_bytes(stage.at[h, others], send_sem.at[1, h])
        wait_bytes(ret[h].at[others], send_sem.at[2, h])
        wait_bytes(back.at[h], send_sem.at[3, h])
        wait_bytes(update.at[:, halves[h]], recv_sem.at[3, h])


def route(*operands):
    grad = operands[3]
    vmem = pl.BlockSpec(memory_space=pltpu.VMEM)
    stat = pltpu.VMEM((BS, BS), jnp.float32)
    square = pltpu.VMEM((BS, BS), jnp.bfloat16)
    return pl.pallas_call(
        route_kernel,
        out_shape=(stat, stat, pltpu.VMEM(grad.shape, jnp.bfloat16)),
        in_specs=[pl.BlockSpec(memory_space=pltpu.HBM)] * 8,
        out_specs=(vmem,) * 3,
        scratch_shapes=[
            pltpu.SMEM((OWNERS,), jnp.int32),
            pltpu.SMEM((NB,), jnp.int32),
            pltpu.SMEM((OWNERS,), jnp.int32),
            pltpu.VMEM(grad.shape, jnp.bfloat16),
            square,
            square,
            pltpu.VMEM((NB, RR, RC), jnp.bfloat16),
            pltpu.VMEM((NB, RR, RC), jnp.bfloat16),
            pltpu.VMEM((2, OWNERS, RR, RC), jnp.bfloat16),
            square,
            pltpu.VMEM((BS, BS), jnp.float32),
            square,
            square,
            pltpu.VMEM((OWNERS, RR, RC), jnp.bfloat16),
            pltpu.VMEM((OWNERS, RR, RC), jnp.bfloat16),
            pltpu.VMEM((2, NB, RR, RC), jnp.bfloat16),
            pltpu.SemaphoreType.DMA((8,)),
            pltpu.SemaphoreType.DMA((4, 2)),
            pltpu.SemaphoreType.DMA((4, 2)),
            pltpu.SemaphoreType.REGULAR((2,)),
        ],
        compiler_params=pltpu.CompilerParams(
            collective_id=0, has_side_effects=True, vmem_limit_bytes=40 * 1024 * 1024
        ),
        cost_estimate=pl.CostEstimate(
            flops=8 * BS**3, bytes_accessed=24 * BS * BS, transcendentals=0
        ),
        name="route",
    )(*(pltpu.with_memory_space_constraint(a, pltpu.HBM) for a in operands))


def write_kernel(left, right, update, left_out, right_out, update_out, sems):
    copies = []
    for src, dst, parts in ((left, left_out, 4), (right, right_out, 4), (update, update_out, 1)):
        rows = src.shape[0] // parts
        for i in range(parts):
            piece = pl.ds(i * rows, rows)
            copies.append(pltpu.make_async_copy(src.at[piece], dst.at[piece], sems.at[len(copies)]))
    for copy in copies:
        copy.start()
    for copy in copies:
        copy.wait()


def write(*arrays):
    return pl.pallas_call(
        write_kernel,
        out_shape=tuple(jax.ShapeDtypeStruct(a.shape, a.dtype) for a in arrays),
        in_specs=[pl.BlockSpec(memory_space=pltpu.VMEM)] * 3,
        out_specs=(pl.BlockSpec(memory_space=pltpu.HBM),) * 3,
        scratch_shapes=[pltpu.SemaphoreType.DMA((9,))],
        compiler_params=pltpu.CompilerParams(vmem_limit_bytes=1024 * 1024),
        cost_estimate=pl.CostEstimate(flops=0, bytes_accessed=18 * BS * BS, transcendentals=0),
        name="write",
    )(*(pltpu.with_memory_space_constraint(a, pltpu.VMEM) for a in arrays))


def body(grad, left_stat, right_stat, left_root, right_root, block_owner, owner_block, owner_count):
    new_left, new_right, update = write(*route(
        owner_block, block_owner, owner_count, grad,
        left_root[0], right_root[0], left_stat[0], right_stat[0],
    ))
    return new_left[None], new_right[None], update


def solution(mesh):
    whole = P(("fsdp", "tp"), None, None)
    return jax.shard_map(
        body,
        mesh=mesh,
        in_specs=(P("fsdp", "tp"), whole, whole, whole, whole, P(), P(), P()),
        out_specs=(whole, whole, P("fsdp", "tp")),
        check_vma=False,
    )
```

time: 96 us -> 90.7 us (0.945)
  Pallas kernels: 95.3 us -> 89.9 us
    pallas_call x1, Pallas kernels: 91.7 us -> 86.3 us  [route(): pl.pallas_call(route_kernel, out_shape=(stat, stat, pltpu.VMEM(grad.shape...]
where the time goes in v3:
time: 90.7 us; the launch traced here: 90.6 us
  Pallas kernels  89.9 us (99%)
    pallas_call x1, Pallas kernels, route(): pl.pallas_call(route_kernel, out_shape=(stat, stat, pltpu.VMEM(grad.shape...  86.3 us
    pallas_call x1, Pallas kernels, write(): pl.pallas_call(write_kernel, out_shape=tuple((jax.ShapeDtypeStruct(a.shap...  3.6 us

profile of v3, /device:TPU:1, one launch (start us, length us, event | category | flops | bytes accessed | tf_op | source)
XLA Modules:
  0.0 90.6 jit_solution(4552864893297751026)
XLA Ops:
  0.6 86.3 %route.1 = (f32[1024,1024]{1,0:T(8,128)S(1)}, f32[1024,1024]{1,0:T(8,128)S(1)}, bf16[384,1024]{1,0:T(8,128)(2,1)S(1)}) custom-call(s32[128]{0:T(128)} %owner_block_any.1, s32[48]{0:T(128)} %block_owner_any.1, s32[128]{0:T(128)} %owner_count_any.1, bf16[384,1024]{1,0:T(8,128)(2,1)} %grad_any.1, bf16[1024,1024]{1,0:T(8,128)(2,1)} %bitcast.10, ...), custom_call_target="tpu_custom_call" | custom-call | flops 8589934592 | bytes 25165824 | tf_op jit(solution)/shard_map/route/pallas_call | solution.py:254
  86.9 3.6 %write.1 = (f32[1024,1024]{1,0:T(8,128)}, f32[1024,1024]{1,0:T(8,128)}, bf16[384,1024]{1,0:T(8,128)(2,1)}) custom-call(f32[1024,1024]{1,0:T(8,128)S(1)} %get-tuple-element.9.left, f32[1024,1024]{1,0:T(8,128)S(1)} %get-tuple-element.10.right, bf16[384,1024]{1,0:T(8,128)(2,1)S(1)} %get-tuple-element.11.update), custom_call_target="tpu_custom_call" | custom-call | bytes 18874368 | tf_op jit(solution)/shard_map/write/pallas_call | solution.py:305

commit v4 on v3

--- a/solution.py
+++ b/solution.py
@@ -119,30 +119,41 @@
     pl.semaphore_wait(heard_sem.at[0], PER)
     tell_targets(heard_sem.at[1])
 
-    for h in range(2):
-        wait_bytes(inter[h], recv_sem.at[0, h])
-        if h == 0:
-            pl.semaphore_wait(heard_sem.at[1], PER)
-        stage[h, me] = inter[h][owner_block[me]]
-        pltpu.make_async_copy(
-            stage.at[h, me], held.at[piece(my_chunk, h, t)], recv_sem.at[1, h]
-        ).start()
-
-        @pl.loop(1, OWNERS)
-        def _(n):
-            m = (n * 37) % OWNERS
-            to_f = ((x + m // 32) % 4) * 2 + (core + m // 16) % 2
-            to_t = shifted_t(t, m % TP)
-            o = to_f * TP + to_t
-            stage[h, o] = inter[h][owner_block[o]]
-            pltpu.make_async_remote_copy(
-                src_ref=stage.at[h, o],
-                dst_ref=held.at[piece(my_chunk, h, t)],
-                send_sem=send_sem.at[1, h],
-                recv_sem=recv_sem.at[1, h],
-                device_id=(to_f, to_t),
-                device_id_type=MESH,
-            ).start()
+    for to_core in range(2):
+        for h in range(2):
+            if to_core == 0:
+                wait_bytes(inter[h], recv_sem.at[0, h])
+                if h == 0:
+                    pl.semaphore_wait(heard_sem.at[1], PER)
+
+            def serve(n):
+                to_f = ((x + n // TP) % 4) * 2 + to_core
+                to_t = shifted_t(t, n % TP)
+                o = to_f * TP + to_t
+                stage[h, o] = inter[h][owner_block[o]]
+                pltpu.make_async_remote_copy(
+                    src_ref=stage.at[h, o],
+                    dst_ref=held.at[piece(my_chunk, h, t)],
+                    send_sem=send_sem.at[1, h],
+                    recv_sem=recv_sem.at[1, h],
+                    device_id=(to_f, to_t),
+                    device_id_type=MESH,
+                ).start()
+
+            @pl.when(core == to_core)
+            def _():
+                stage[h, me] = inter[h][owner_block[me]]
+                pltpu.make_async_copy(
+                    stage.at[h, me], held.at[piece(my_chunk, h, t)], recv_sem.at[1, h]
+                ).start()
+
+            @pl.when(core != to_core)
+            def _():
+                serve(0)
+
+            @pl.loop(1, OWNERS // 2)
+            def _(n):
+                serve((n * 37) % (OWNERS // 2))
 
     fetches[4].wait()
     fetches[5].wait()

time: 90.7 us -> 84 us (0.926)
  Pallas kernels: 89.9 us -> 83.2 us
    pallas_call x1, Pallas kernels: 86.3 us -> 79.6 us  [route(): pl.pallas_call(route_kernel, out_shape=(stat, stat, pltpu.VMEM(grad.shape...]
where the time goes in v4:
time: 84 us; the launch traced here: 83.9 us
  Pallas kernels  83.2 us (99%)
    pallas_call x1, Pallas kernels, route(): pl.pallas_call(route_kernel, out_shape=(stat, stat, pltpu.VMEM(grad.shape...  79.6 us
    pallas_call x1, Pallas kernels, write(): pl.pallas_call(write_kernel, out_shape=tuple((jax.ShapeDtypeStruct(a.shap...  3.6 us

profile of v4, /device:TPU:1, one launch (start us, length us, event | category | flops | bytes accessed | tf_op | source)
XLA Modules:
  0.0 83.9 jit_solution(16964449872459672454)
XLA Ops:
  0.6 79.6 %route.1 = (f32[1024,1024]{1,0:T(8,128)S(1)}, f32[1024,1024]{1,0:T(8,128)S(1)}, bf16[384,1024]{1,0:T(8,128)(2,1)S(1)}) custom-call(s32[128]{0:T(128)} %owner_block_any.1, s32[48]{0:T(128)} %block_owner_any.1, s32[128]{0:T(128)} %owner_count_any.1, bf16[384,1024]{1,0:T(8,128)(2,1)} %grad_any.1, bf16[1024,1024]{1,0:T(8,128)(2,1)} %bitcast.10, ...), custom_call_target="tpu_custom_call" | custom-call | flops 8589934592 | bytes 25165824 | tf_op jit(solution)/shard_map/route/pallas_call | solution.py:265
  80.3 3.6 %write.1 = (f32[1024,1024]{1,0:T(8,128)}, f32[1024,1024]{1,0:T(8,128)}, bf16[384,1024]{1,0:T(8,128)(2,1)}) custom-call(f32[1024,1024]{1,0:T(8,128)S(1)} %get-tuple-element.9.left, f32[1024,1024]{1,0:T(8,128)S(1)} %get-tuple-element.10.right, bf16[384,1024]{1,0:T(8,128)(2,1)S(1)} %get-tuple-element.11.update), custom_call_target="tpu_custom_call" | custom-call | bytes 18874368 | tf_op jit(solution)/shard_map/write/pallas_call | solution.py:316

commit v5 on v4

v5 whole, which is shorter than its diff:
```python
import jax
import jax.numpy as jnp
from jax import lax
from jax.experimental import pallas as pl
from jax.experimental.pallas import tpu as pltpu
from jax.sharding import PartitionSpec as P

MESH = pl.DeviceIdType.MESH
BS = 1024
FS = 8
TP = 16
NB = 48
OWNERS = FS * TP
CHUNK = BS // FS
PER = 3
STEP = 256
RR = 16
IN = (512, 512)
OUT = (768, 256)


def part_cols(parts, h):
    return pl.ds(sum(parts[:h]), parts[h])


def piece(chunk, parts, h, t):
    width = parts[h] // 2
    return (
        pl.ds(pl.multiple_of(chunk * CHUNK + lax.div(t, 2) * RR, RR), RR),
        pl.ds(pl.multiple_of(sum(parts[:h]) + lax.rem(t, 2) * width, 128), width),
    )


def swapped(k):
    return lax.div(k, 4) * 4 + 3 - lax.rem(k, 4)


def shifted_t(t, n):
    y = lax.rem(lax.div(t, 4) + lax.div(n, 4), 4)
    return y * 4 + lax.rem(t + n, 4)


def wait_bytes(ref, sem):
    pltpu.make_async_copy(ref, ref, sem).wait()


def steps(parts, h):
    def over(fn):
        first = sum(parts[:h]) // STEP

        @pl.loop(first, first + parts[h] // STEP)
        def _(c):
            fn(pl.ds(pl.multiple_of(c * STEP, STEP), STEP))

    return over


def route_kernel(
    owner_block_any, block_owner_any, owner_count_any, grad_any,
    left_root_any, right_root_any, left_stat_any, right_stat_any,
    new_left, new_right, update,
    owner_block, block_owner, owner_count, grad, left_root, right_root,
    inter_0, inter_1, stage_0, stage_1, held, total, mixed, done, ret_0, ret_1, back_0, back_1,
    local_sem, send_sem, recv_sem, heard_sem,
):
    f = lax.axis_index("fsdp")
    t = lax.axis_index("tp")
    me = f * TP + t
    x, core = f // 2, f % 2
    my_chunk = swapped(f)
    inter, stage = (inter_0, inter_1), (stage_0, stage_1)
    ret, back = (ret_0, ret_1), (back_0, back_1)

    fetches = [
        pltpu.make_async_copy(src, dst, local_sem.at[i])
        for i, (src, dst) in enumerate((
            (owner_block_any, owner_block),
            (block_owner_any, block_owner),
            (owner_count_any, owner_count),
            (grad_any, grad),
            (left_root_any, left_root),
            (right_root_any, right_root),
            (left_stat_any, new_left),
            (right_stat_any, new_right),
        ))
    ]
    fetches[3].start()

    targets = [swapped((f * PER + q) % FS) for q in range(PER)]
    sources = [(band * FS + my_chunk) // PER for band in range(PER)]
    spread_to = [(f * PER + q) // FS * TP + t for q in range(PER)]
    barrier = pltpu.get_barrier_semaphore()

    for band in range(PER):
        for n in range(TP):
            pl.semaphore_signal(
                barrier, inc=1, device_id=(sources[band], (t + n) % TP), device_id_type=MESH
            )

    fetches[3].wait()
    pl.semaphore_wait(barrier, PER * TP)

    def tell_targets(sem):
        for to_f in targets:
            pl.semaphore_signal(sem, inc=1, device_id=(to_f, t), device_id_type=MESH)

    tell_targets(heard_sem.at[0])

    for h in range(2):
        @pl.loop(0, TP)
        def _(n):
            to_t = shifted_t(t, lax.rem(n * 5, TP))
            for q in range(PER):
                pltpu.make_async_remote_copy(
                    src_ref=grad.at[piece(q, IN, h, to_t)],
                    dst_ref=inter[h].at[spread_to[q]],
                    send_sem=send_sem.at[0, h],
                    recv_sem=recv_sem.at[0, h],
                    device_id=(targets[q], to_t),
                    device_id_type=MESH,
                ).start()

    for i in (0, 1, 2, 4, 5, 6, 7):
        fetches[i].start()

    pl.semaphore_wait(heard_sem.at[0], PER)
    tell_targets(heard_sem.at[1])
    for fetch in fetches[:3]:
        fetch.wait()

    for to_core in range(2):
        for h in range(2):
            if to_core == 0:
                wait_bytes(inter[h], recv_sem.at[0, h])
                if h == 0:
                    pl.semaphore_wait(heard_sem.at[1], PER)

            def serve(n):
                to_f = lax.rem(x + lax.div(n, TP), 4) * 2 + to_core
                to_t = shifted_t(t, lax.rem(n, TP))
                o = to_f * TP + to_t
                stage[h][o] = inter[h][owner_block[o]]
                pltpu.make_async_remote_copy(
                    src_ref=stage[h].at[o],
                    dst_ref=held.at[piece(my_chunk, IN, h, t)],
                    send_sem=send_sem.at[1, h],
                    recv_sem=recv_sem.at[1, h],
                    device_id=(to_f, to_t),
                    device_id_type=MESH,
                ).start()

            @pl.when(core == to_core)
            def _():
                stage[h][me] = inter[h][owner_block[me]]
                pltpu.make_async_copy(
                    stage[h].at[me], held.at[piece(my_chunk, IN, h, t)], recv_sem.at[1, h]
                ).start()

            @pl.when(core != to_core)
            def _():
                serve(jnp.int32(0))

            @pl.loop(1, OWNERS // 2)
            def _(n):
                serve(lax.rem(n * 37, OWNERS // 2))

    fetches[4].wait()
    fetches[5].wait()

    def mix(h):
        @steps(IN, h)
        def _(cols):
            mixed[:, cols] = jnp.dot(
                left_root[...], held[:, cols], preferred_element_type=jnp.float32
            ).astype(jnp.bfloat16)

    def finish(h, cols):
        rows = part_cols(IN, h)
        return jnp.dot(
            mixed[:, rows], right_root[rows, cols], preferred_element_type=jnp.float32
        )

    wait_bytes(held.at[:, part_cols(IN, 0)], recv_sem.at[1, 0])
    mix(0)

    @steps((BS,), 0)
    def _(cols):
        total[:, cols] = finish(0, cols)

    wait_bytes(held.at[:, part_cols(IN, 1)], recv_sem.at[1, 1])
    mix(1)

    for h in range(2):
        @steps(OUT, h)
        def _(cols):
            done[:, cols] = (total[:, cols] + finish(1, cols)).astype(jnp.bfloat16)

        pltpu.make_async_copy(
            done.at[piece(my_chunk, OUT, h, t)], ret[h].at[me], recv_sem.at[2, h]
        ).start()

        @pl.loop(1, OWNERS)
        def _(n):
            m = lax.rem(n * 37, OWNERS)
            to_f = lax.rem(x + lax.div(m, 32), 4) * 2 + lax.rem(core + lax.div(m, TP), 2)
            to_t = shifted_t(t, lax.rem(m, TP))
            pltpu.make_async_remote_copy(
                src_ref=done.at[piece(swapped(to_f), OUT, h, to_t)],
                dst_ref=ret[h].at[me],
                send_sem=send_sem.at[2, h],
                recv_sem=recv_sem.at[2, h],
                device_id=(to_f, to_t),
                device_id_type=MESH,
            ).start()

    count = owner_count[me].astype(jnp.float32)

    def add_statistics():
        for sem, stat, axis in ((7, new_right, 0), (6, new_left, 1)):
            fetches[sem].wait()

            @steps((BS,), 0)
            def _(some):
                lhs = held[:, some] if axis == 0 else held[some, :]
                stat[some, :] += count * lax.dot_general(
                    lhs, held[...], (((axis,), (axis,)), ((), ())),
                    preferred_element_type=jnp.float32,
                )

    pl.when(core == 0)(add_statistics)

    for h in range(2):
        wait_bytes(ret[h], recv_sem.at[2, h])

        @pl.loop(0, TP)
        def _(n):
            to_t = shifted_t(t, lax.rem(n * 5, TP))
            for band in range(PER):
                b = band * TP + to_t
                back[h][b] = ret[h][block_owner[b]]
                pltpu.make_async_remote_copy(
                    src_ref=back[h].at[b],
                    dst_ref=update.at[piece((band * FS + my_chunk) % PER, OUT, h, t)],
                    send_sem=send_sem.at[3, h],
                    recv_sem=recv_sem.at[3, h],
                    device_id=(sources[band], to_t),
                    device_id_type=MESH,
                ).start()

    pl.when(core == 1)(add_statistics)

    others = pl.ds(0, OWNERS - 1)
    for h in range(2):
        wait_bytes(inter[h], send_sem.at[0, h])
        wait_bytes(stage[h].at[others], send_sem.at[1, h])
        wait_bytes(ret[h].at[others], send_sem.at[2, h])
        wait_bytes(back[h], send_sem.at[3, h])
        wait_bytes(update.at[:, part_cols(OUT, h)], recv_sem.at[3, h])


def route(*operands):
    grad = operands[3]
    vmem = pl.BlockSpec(memory_space=pltpu.VMEM)
    stat = pltpu.VMEM((BS, BS), jnp.float32)
    square = pltpu.VMEM((BS, BS), jnp.bfloat16)
    return pl.pallas_call(
        route_kernel,
        out_shape=(stat, stat, pltpu.VMEM(grad.shape, jnp.bfloat16)),
        in_specs=[pl.BlockSpec(memory_space=pltpu.HBM)] * 8,
        out_specs=(vmem,) * 3,
        scratch_shapes=[
            pltpu.SMEM((OWNERS,), jnp.int32),
            pltpu.SMEM((NB,), jnp.int32),
            pltpu.SMEM((OWNERS,), jnp.int32),
            pltpu.VMEM(grad.shape, jnp.bfloat16),
            square,
            square,
            *[pltpu.VMEM((NB, RR, w // 2), jnp.bfloat16) for w in IN],
            *[pltpu.VMEM((OWNERS, RR, w // 2), jnp.bfloat16) for w in IN],
            square,
            pltpu.VMEM((BS, BS), jnp.float32),
            square,
            square,
            *[pltpu.VMEM((OWNERS, RR, w // 2), jnp.bfloat16) for w in OUT],
            *[pltpu.VMEM((NB, RR, w // 2), jnp.bfloat16) for w in OUT],
            pltpu.SemaphoreType.DMA((8,)),
            pltpu.SemaphoreType.DMA((4, 2)),
            pltpu.SemaphoreType.DMA((4, 2)),
            pltpu.SemaphoreType.REGULAR((2,)),
        ],
        compiler_params=pltpu.CompilerParams(
            collective_id=0, has_side_effects=True, vmem_limit_bytes=40 * 1024 * 1024
        ),
        cost_estimate=pl.CostEstimate(
            flops=8 * BS**3, bytes_accessed=24 * BS * BS, transcendentals=0
        ),
        name="route",
    )(*(pltpu.with_memory_space_constraint(a, pltpu.HBM) for a in operands))


def write_kernel(left, right, update, left_out, right_out, update_out, sems):
    copies = []
    for src, dst, parts in ((left, left_out, 4), (right, right_out, 4), (update, update_out, 1)):
        rows = src.shape[0] // parts
        for i in range(parts):
            piece = pl.ds(i * rows, rows)
            copies.append(pltpu.make_async_copy(src.at[piece], dst.at[piece], sems.at[len(copies)]))
    for copy in copies:
        copy.start()
    for copy in copies:
        copy.wait()


def write(*arrays):
    return pl.pallas_call(
        write_kernel,
        out_shape=tuple(jax.ShapeDtypeStruct(a.shape, a.dtype) for a in arrays),
        in_specs=[pl.BlockSpec(memory_space=pltpu.VMEM)] * 3,
        out_specs=(pl.BlockSpec(memory_space=pltpu.HBM),) * 3,
        scratch_shapes=[pltpu.SemaphoreType.DMA((9,))],
        compiler_params=pltpu.CompilerParams(vmem_limit_bytes=1024 * 1024),
        cost_estimate=pl.CostEstimate(flops=0, bytes_accessed=18 * BS * BS, transcendentals=0),
        name="write",
    )(*(pltpu.with_memory_space_constraint(a, pltpu.VMEM) for a in arrays))


def body(grad, left_stat, right_stat, left_root, right_root, block_owner, owner_block, owner_count):
    new_left, new_right, update = write(*route(
        owner_block, block_owner, owner_count, grad,
        left_root[0], right_root[0], left_stat[0], right_stat[0],
    ))
    return new_left[None], new_right[None], update


def solution(mesh):
    whole = P(("fsdp", "tp"), None, None)
    return jax.shard_map(
        body,
        mesh=mesh,
        in_specs=(P("fsdp", "tp"), whole, whole, whole, whole, P(), P(), P()),
        out_specs=(whole, whole, P("fsdp", "tp")),
        check_vma=False,
    )
```

time: 84 us -> 81.9 us (0.975)
  Pallas kernels: 83.2 us -> 81.1 us
    pallas_call x1, Pallas kernels: 79.6 us -> 77.5 us  [route(): pl.pallas_call(route_kernel, out_shape=(stat, stat, pltpu.VMEM(grad.shape...]
where the time goes in v5:
time: 81.9 us; the launch traced here: 81.8 us
  Pallas kernels  81.1 us (99%)
    pallas_call x1, Pallas kernels, route(): pl.pallas_call(route_kernel, out_shape=(stat, stat, pltpu.VMEM(grad.shape...  77.5 us
    pallas_call x1, Pallas kernels, write(): pl.pallas_call(write_kernel, out_shape=tuple((jax.ShapeDtypeStruct(a.shap...  3.6 us

profile of v5, /device:TPU:1, one launch (start us, length us, event | category | flops | bytes accessed | tf_op | source)
XLA Modules:
  0.0 81.8 jit_solution(1846700563907147641)
XLA Ops:
  0.6 77.5 %route.1 = (f32[1024,1024]{1,0:T(8,128)S(1)}, f32[1024,1024]{1,0:T(8,128)S(1)}, bf16[384,1024]{1,0:T(8,128)(2,1)S(1)}) custom-call(s32[128]{0:T(128)} %owner_block_any.1, s32[48]{0:T(128)} %block_owner_any.1, s32[128]{0:T(128)} %owner_count_any.1, bf16[384,1024]{1,0:T(8,128)(2,1)} %grad_any.1, bf16[1024,1024]{1,0:T(8,128)(2,1)} %bitcast.10, ...), custom_call_target="tpu_custom_call" | custom-call | flops 8589934592 | bytes 25165824 | tf_op jit(solution)/shard_map/route/pallas_call | solution.py:266
  78.2 3.6 %write.1 = (f32[1024,1024]{1,0:T(8,128)}, f32[1024,1024]{1,0:T(8,128)}, bf16[384,1024]{1,0:T(8,128)(2,1)}) custom-call(f32[1024,1024]{1,0:T(8,128)S(1)} %get-tuple-element.9.left, f32[1024,1024]{1,0:T(8,128)S(1)} %get-tuple-element.10.right, bf16[384,1024]{1,0:T(8,128)(2,1)S(1)} %get-tuple-element.11.update), custom_call_target="tpu_custom_call" | custom-call | bytes 18874368 | tf_op jit(solution)/shard_map/write/pallas_call | solution.py:315

commit v6 on v5

--- a/solution.py
+++ b/solution.py
@@ -162,7 +162,7 @@
 
             @pl.loop(1, OWNERS // 2)
             def _(n):
-                serve(lax.rem(n * 37, OWNERS // 2))
+                serve(lax.rem(n * 53, OWNERS // 2))
 
     fetches[4].wait()
     fetches[5].wait()
@@ -201,7 +201,7 @@
 
         @pl.loop(1, OWNERS)
         def _(n):
-            m = lax.rem(n * 37, OWNERS)
+            m = lax.rem(n * 69, OWNERS)
             to_f = lax.rem(x + lax.div(m, 32), 4) * 2 + lax.rem(core + lax.div(m, TP), 2)
             to_t = shifted_t(t, lax.rem(m, TP))
             pltpu.make_async_remote_copy(

time: 81.9 us -> 81.1 us (level)
  no operation moved by 1% of the time
where the time goes in v6:
time: 81.1 us; the launch traced here: 81 us
  Pallas kernels  80.3 us (99%)
    pallas_call x1, Pallas kernels, route(): pl.pallas_call(route_kernel, out_shape=(stat, stat, pltpu.VMEM(grad.shape...  76.7 us
    pallas_call x1, Pallas kernels, write(): pl.pallas_call(write_kernel, out_shape=tuple((jax.ShapeDtypeStruct(a.shap...  3.6 us

profile of v6, /device:TPU:1, one launch (start us, length us, event | category | flops | bytes accessed | tf_op | source)
XLA Modules:
  0.0 81.0 jit_solution(5997700111066602149)
XLA Ops:
  0.6 76.7 %route.1 = (f32[1024,1024]{1,0:T(8,128)S(1)}, f32[1024,1024]{1,0:T(8,128)S(1)}, bf16[384,1024]{1,0:T(8,128)(2,1)S(1)}) custom-call(s32[128]{0:T(128)} %owner_block_any.1, s32[48]{0:T(128)} %block_owner_any.1, s32[128]{0:T(128)} %owner_count_any.1, bf16[384,1024]{1,0:T(8,128)(2,1)} %grad_any.1, bf16[1024,1024]{1,0:T(8,128)(2,1)} %bitcast.10, ...), custom_call_target="tpu_custom_call" | custom-call | flops 8589934592 | bytes 25165824 | tf_op jit(solution)/shard_map/route/pallas_call | solution.py:266
  77.3 3.6 %write.1 = (f32[1024,1024]{1,0:T(8,128)}, f32[1024,1024]{1,0:T(8,128)}, bf16[384,1024]{1,0:T(8,128)(2,1)}) custom-call(f32[1024,1024]{1,0:T(8,128)S(1)} %get-tuple-element.9.left, f32[1024,1024]{1,0:T(8,128)S(1)} %get-tuple-element.10.right, bf16[384,1024]{1,0:T(8,128)(2,1)S(1)} %get-tuple-element.11.update), custom_call_target="tpu_custom_call" | custom-call | bytes 18874368 | tf_op jit(solution)/shard_map/write/pallas_call | solution.py:315

commit v7 on v6

--- a/solution.py
+++ b/solution.py
@@ -56,10 +56,10 @@
 
 
 def route_kernel(
-    owner_block_any, block_owner_any, owner_count_any, grad_any,
+    owner_block_any, block_owner_any, owner_count_any, grad,
     left_root_any, right_root_any, left_stat_any, right_stat_any,
     new_left, new_right, update,
-    owner_block, block_owner, owner_count, grad, left_root, right_root,
+    owner_block, block_owner, owner_count, left_root, right_root,
     inter_0, inter_1, stage_0, stage_1, held, total, mixed, done, ret_0, ret_1, back_0, back_1,
     local_sem, send_sem, recv_sem, heard_sem,
 ):
@@ -77,14 +77,12 @@
             (owner_block_any, owner_block),
             (block_owner_any, block_owner),
             (owner_count_any, owner_count),
-            (grad_any, grad),
             (left_root_any, left_root),
             (right_root_any, right_root),
             (left_stat_any, new_left),
             (right_stat_any, new_right),
         ))
     ]
-    fetches[3].start()
 
     targets = [swapped((f * PER + q) % FS) for q in range(PER)]
     sources = [(band * FS + my_chunk) // PER for band in range(PER)]
@@ -97,7 +95,6 @@
                 barrier, inc=1, device_id=(sources[band], (t + n) % TP), device_id_type=MESH
             )
 
-    fetches[3].wait()
     pl.semaphore_wait(barrier, PER * TP)
 
     def tell_targets(sem):
@@ -120,8 +117,8 @@
                     device_id_type=MESH,
                 ).start()
 
-    for i in (0, 1, 2, 4, 5, 6, 7):
-        fetches[i].start()
+    for fetch in fetches:
+        fetch.start()
 
     pl.semaphore_wait(heard_sem.at[0], PER)
     tell_targets(heard_sem.at[1])
@@ -164,8 +161,8 @@
             def _(n):
                 serve(lax.rem(n * 53, OWNERS // 2))
 
+    fetches[3].wait()
     fetches[4].wait()
-    fetches[5].wait()
 
     def mix(h):
         @steps(IN, h)
@@ -216,7 +213,7 @@
     count = owner_count[me].astype(jnp.float32)
 
     def add_statistics():
-        for sem, stat, axis in ((7, new_right, 0), (6, new_left, 1)):
+        for sem, stat, axis in ((6, new_right, 0), (5, new_left, 1)):
             fetches[sem].wait()
 
             @steps((BS,), 0)
@@ -272,7 +269,6 @@
             pltpu.SMEM((OWNERS,), jnp.int32),
             pltpu.SMEM((NB,), jnp.int32),
             pltpu.SMEM((OWNERS,), jnp.int32),
-            pltpu.VMEM(grad.shape, jnp.bfloat16),
             square,
             square,
             *[pltpu.VMEM((NB, RR, w // 2), jnp.bfloat16) for w in IN],
@@ -283,7 +279,7 @@
             square,
             *[pltpu.VMEM((OWNERS, RR, w // 2), jnp.bfloat16) for w in OUT],
             *[pltpu.VMEM((NB, RR, w // 2), jnp.bfloat16) for w in OUT],
-            pltpu.SemaphoreType.DMA((8,)),
+            pltpu.SemaphoreType.DMA((7,)),
             pltpu.SemaphoreType.DMA((4, 2)),
             pltpu.SemaphoreType.DMA((4, 2)),
             pltpu.SemaphoreType.REGULAR((2,)),

time: 81.1 us -> 81.3 us (level)
  no operation moved by 1% of the time
where the time goes in v7:
time: 81.3 us; the launch traced here: 81.2 us
  Pallas kernels  80.5 us (99%)
    pallas_call x1, Pallas kernels, route(): pl.pallas_call(route_kernel, out_shape=(stat, stat, pltpu.VMEM(grad.shape...  76.9 us
    pallas_call x1, Pallas kernels, write(): pl.pallas_call(write_kernel, out_shape=tuple((jax.ShapeDtypeStruct(a.shap...  3.6 us

profile of v7, /device:TPU:1, one launch (start us, length us, event | category | flops | bytes accessed | tf_op | source)
XLA Modules:
  0.0 81.2 jit_solution(1284295953697569185)
XLA Ops:
  0.6 76.9 %route.1 = (f32[1024,1024]{1,0:T(8,128)S(1)}, f32[1024,1024]{1,0:T(8,128)S(1)}, bf16[384,1024]{1,0:T(8,128)(2,1)S(1)}) custom-call(s32[128]{0:T(128)} %owner_block_any.1, s32[48]{0:T(128)} %block_owner_any.1, s32[128]{0:T(128)} %owner_count_any.1, bf16[384,1024]{1,0:T(8,128)(2,1)} %grad.1, bf16[1024,1024]{1,0:T(8,128)(2,1)} %bitcast.10, ...), custom_call_target="tpu_custom_call" | custom-call | flops 8589934592 | bytes 25165824 | tf_op jit(solution)/shard_map/route/pallas_call | solution.py:263
  77.6 3.6 %write.1 = (f32[1024,1024]{1,0:T(8,128)}, f32[1024,1024]{1,0:T(8,128)}, bf16[384,1024]{1,0:T(8,128)(2,1)}) custom-call(f32[1024,1024]{1,0:T(8,128)S(1)} %get-tuple-element.9.left, f32[1024,1024]{1,0:T(8,128)S(1)} %get-tuple-element.10.right, bf16[384,1024]{1,0:T(8,128)(2,1)S(1)} %get-tuple-element.11.update), custom_call_target="tpu_custom_call" | custom-call | bytes 18874368 | tf_op jit(solution)/shard_map/write/pallas_call | solution.py:311
